TPU v7x, 32 devices: a whole 2x2x4 slice. The times are simulated.
32 devices in a mesh: groups: 2 (over x), gx: 4 (over y, core), gy: 4 (over z).
Axes of the slice: x: 2, y: 2, z: 4, core: 2. Of those that a mesh axis runs over, the one named last changes fastest.
Arguments:
- tokens: bfloat16 [1024, 6144], P(('groups', 'gy'), 'gx'), parts along dimension 0, may hold values from -6 to 6
- w_in: bfloat16 [6144, 24576], P('gx', 'gy'), may hold values from -0.078125 to 0.078125
- w_out: bfloat16 [24576, 6144], P('gy', 'gx'), may hold values from -0.0390625 to 0.0390625
- grad_out: bfloat16 [1024, 6144], P(('groups', 'gy'), 'gx'), parts along dimension 0, may hold values from -1.1953125 to 1.1953125
Outputs:
- output: bfloat16 [1024, 6144], P(('groups', 'gy'), 'gx'), parts along dimension 0
- grad_tokens: bfloat16 [1024, 6144], P(('groups', 'gy'), 'gx'), parts along dimension 0
- grad_w_in: bfloat16 [12288, 24576], P(('groups', 'gx'), 'gy'), parts along dimension 0
- grad_w_out: bfloat16 [49152, 6144], P(('groups', 'gy'), 'gx'), parts along dimension 0
There are 2 independent parts, one for each index of `groups`. A program takes and returns all parts, laid end to end along the dimension named above; an argument that names none is the same for every part. Nothing has to cross between parts.
All inputs are finite; a program needn't handle non-finite values.
Results may differ from a plain program's by a relative error of at most 0.018.
Values may be sent and summed in bfloat16 or wider, within the bound.
A program may use at most 192 MiB of HBM per device.

v0:
```python
import jax
import jax.numpy as jnp
from jax import lax
from jax.sharding import PartitionSpec as P


def gelu_slope(value):
    coeff = 0.7978845608028654
    inner = coeff * (value + 0.044715 * value * value * value)
    tanh_val = jnp.tanh(inner)
    return 0.5 * (1.0 + tanh_val) + 0.5 * value * (1.0 - tanh_val * tanh_val) * coeff * (
        1.0 + 3.0 * 0.044715 * value * value
    )


def product(left_mat, right_mat, flipped):
    if flipped:
        return lax.dot_general(
            left_mat, right_mat, (((1,), (1,)), ((), ())), preferred_element_type=jnp.float32
        )
    return jnp.dot(left_mat, right_mat, preferred_element_type=jnp.float32)


def inner_rows(left_mat, right_mat):
    return lax.dot_general(
        left_mat, right_mat, (((0,), (0,)), ((), ())), preferred_element_type=jnp.float32
    )


def token_gather(local_rows):
    return lax.all_gather(local_rows, "gy", axis=0, tiled=True)


def token_total(term):
    return lax.psum_scatter(term.astype(jnp.bfloat16), "gy", scatter_dimension=0, tiled=True)


def shards(tokens, w_in, w_out, grad_out):

    def hidden_sum(left_mat, right_mat, flipped):
        return lax.psum_scatter(
            product(left_mat, right_mat, flipped).astype(jnp.bfloat16),
            "gx",
            scatter_dimension=1,
            tiled=True,
        ).astype(jnp.float32)

    def hidden_gather(share_part):
        return lax.all_gather(share_part, "gx", axis=1, tiled=True)

    rows_in = token_gather(tokens)
    pre_act = hidden_sum(rows_in, w_in, False)
    hidden = jax.nn.gelu(pre_act, approximate=True).astype(jnp.bfloat16)
    hidden_all = hidden_gather(hidden)
    output = token_total(product(hidden_all, w_out, False))
    grads_in = token_gather(grad_out)
    grad_hidden = hidden_sum(grads_in, w_out, True)
    grad_pre = (grad_hidden * gelu_slope(pre_act)).astype(jnp.bfloat16)
    grad_all = hidden_gather(grad_pre)
    grad_w_out = inner_rows(hidden_all, grads_in).astype(jnp.bfloat16)
    grad_w_in = inner_rows(rows_in, grad_all).astype(jnp.bfloat16)
    grad_tokens = token_total(product(grad_all, w_in, True))
    return (output, grad_tokens, grad_w_in, grad_w_out)


def solution(mesh):
    in_specs = (P(("groups", "gy"), "gx"), P("gx", "gy"), P("gy", "gx"), P(("groups", "gy"), "gx"))
    out_specs = (
        P(("groups", "gy"), "gx"),
        P(("groups", "gy"), "gx"),
        P(("groups", "gx"), "gy"),
        P(("groups", "gy"), "gx"),
    )
    return jax.shard_map(shards, mesh=mesh, in_specs=in_specs, out_specs=out_specs, check_vma=False)
```

profile of v0, /device:TPU:0, one launch (start us, length us, event | category | flops | bytes accessed | tf_op | source)
XLA Modules:
  0.0 391.7 jit_solution(9756797595313594828)
XLA Ops:
  7.2 0.0 all-gather.9.cloned.1.call-start
  7.2 0.7 all-gather.9.cloned.1.call-update
  7.9 0.0 all-gather.5.cloned.1.call-start
  7.9 0.7 all-gather.5.cloned.1.call-update
  8.6 0.0 reduce-scatter.9.cloned.1.call-start
  8.7 40.7 %all-gather.9.cloned.1.call-done = bf16[512,1536]{1,0:T(8,128)(2,1)} async-done(((bf16[128,1536]{1,0:T(8,128)(2,1)}), bf16[512,1536]{1,0:T(8,128)(2,1)}) %all-gather.9.cloned.1.call-update) | async-done | bytes 1572880 | tf_op jit(solution)/shard_map/all_gather | solution.py:31
  49.4 15.9 %convolution_convert_fusion.2 = bf16[512,6144]{1,0:T(8,128)(2,1)} fusion(bf16[512,1536]{1,0:T(8,128)(2,1)} %all-gather.9.cloned.1.call-done, bf16[6144,1536]{1,0:T(8,128)(2,1)} %param.6), kind=kOutput, calls=%fused_computation.14 | convolution fusion | flops 9666822144 | bytes 26738688 | tf_op jit(solution)/shard_map/dot_general | solution.py:18
  65.3 0.0 reduce-scatter.9.cloned.1.call-update
  65.3 0.0 reduce-scatter.5.cloned.1.call-start
  65.4 21.6 %all-gather.5.cloned.1.call-done = bf16[512,1536]{1,0:T(8,128)(2,1)} async-done(((bf16[128,1536]{1,0:T(8,128)(2,1)}), bf16[512,1536]{1,0:T(8,128)(2,1)}) %all-gather.5.cloned.1.call-update) | async-done | bytes 1572880 | tf_op jit(solution)/shard_map/all_gather | solution.py:31
  87.0 15.9 %convolution_convert_fusion.3 = bf16[512,6144]{1,0:T(8,128)(2,1)} fusion(bf16[512,1536]{1,0:T(8,128)(2,1)} %all-gather.5.cloned.1.call-done, bf16[1536,6144]{1,0:T(8,128)(2,1)} %param.5), kind=kOutput, calls=%fused_computation.15 | convolution fusion | flops 9666822144 | bytes 26738688 | tf_op jit(solution)/shard_map/dot_general | solution.py:21
  102.8 0.0 reduce-scatter.5.cloned.1.call-update
  102.8 0.0 all-gather.7.cloned.1.call-start
  102.9 44.5 %reduce-scatter.9.cloned.1.call-done = bf16[512,1536]{1,0:T(8,128)(2,1)} async-done(((bf16[512,6144]{1,0:T(8,128)(2,1)}), bf16[512,1536]{1,0:T(8,128)(2,1)}) %reduce-scatter.9.cloned.1.call-update) | async-done | bytes 1572880 | tf_op jit(solution)/shard_map/reduce_scatter | solution.py:41
  147.3 61.5 %reduce-scatter.5.cloned.1.call-done = bf16[512,1536]{1,0:T(8,128)(2,1)} async-done(((bf16[512,6144]{1,0:T(8,128)(2,1)}), bf16[512,1536]{1,0:T(8,128)(2,1)}) %reduce-scatter.5.cloned.1.call-update) | async-done | bytes 1572880 | tf_op jit(solution)/shard_map/reduce_scatter | solution.py:41
  208.9 5.7 %fusion.14 = (bf16[512,1536]{1,0:T(8,128)(2,1)}, bf16[512,1536]{1,0:T(8,128)(2,1)}) fusion(bf16[512,1536]{1,0:T(8,128)(2,1)} %reduce-scatter.5.cloned.1.call-done, bf16[512,1536]{1,0:T(8,128)(2,1)} %reduce-scatter.9.cloned.1.call-done), kind=kLoop, calls=%fused_computation.29 | loop fusion | flops 23592960 | bytes 6291456 | tf_op jit(solution)/shard_map/convert_element_type | solution.py:58
  214.5 0.0 all-gather.7.cloned.1.call-update
  214.6 0.0 all-gather.11.cloned.1.call-start
  214.6 0.5 all-gather.11.cloned.1.call-update
  215.2 0.2 reduce-scatter.7.cloned.1.call-start
  215.4 45.7 %all-gather.7.cloned.1.call-done = bf16[512,6144]{1,0:T(8,128)(2,1)} async-done(((bf16[512,1536]{1,0:T(8,128)(2,1)}), bf16[512,6144]{1,0:T(8,128)(2,1)}) %all-gather.7.cloned.1.call-update) | async-done | bytes 6291472 | tf_op jit(solution)/shard_map/all_gather | solution.py:49
  261.1 16.7 %convolution_convert_fusion.5 = bf16[512,1536]{1,0:T(8,128)(2,1)} fusion(bf16[512,6144]{1,0:T(8,128)(2,1)} %all-gather.7.cloned.1.call-done, bf16[6144,1536]{1,0:T(8,128)(2,1)} %param.6), kind=kOutput, calls=%fused_computation.32 | convolution fusion | flops 9664462848 | bytes 26738688 | tf_op jit(solution)/shard_map/dot_general | solution.py:21
  277.8 0.0 reduce-scatter.7.cloned.1.call-update
  277.8 0.0 copy-start.1
  277.8 0.0 reduce-scatter.11.cloned.1.call-start
  277.9 31.7 %all-gather.11.cloned.1.call-done = bf16[512,6144]{1,0:T(8,128)(2,1)} async-done(((bf16[512,1536]{1,0:T(8,128)(2,1)}), bf16[512,6144]{1,0:T(8,128)(2,1)}) %all-gather.11.cloned.1.call-update) | async-done | bytes 6291472 | tf_op jit(solution)/shard_map/all_gather | solution.py:49
  309.5 16.6 %convolution_convert_fusion.4 = bf16[512,1536]{1,0:T(8,128)(2,1)} fusion(bf16[512,6144]{1,0:T(8,128)(2,1)} %all-gather.11.cloned.1.call-done, bf16[1536,6144]{1,0:T(8,128)(2,1)} %param.5), kind=kOutput, calls=%fused_computation.31 | convolution fusion | flops 9664462848 | bytes 26738688 | tf_op jit(solution)/shard_map/dot_general | solution.py:18
  326.1 0.0 reduce-scatter.11.cloned.1.call-update
  326.2 16.0 %fusion = bf16[1536,6144]{0,1:T(8,128)(2,1)} fusion(bf16[512,6144]{1,0:T(8,128)(2,1)} %all-gather.11.cloned.1.call-done, bf16[512,1536]{1,0:T(8,128)(2,1)S(1)} %copy-done.1), kind=kOutput, calls=%fused_computation.2 | convolution fusion | flops 9673113600 | bytes 26738688 | tf_op jit(solution)/shard_map/dot_general | solution.py:25
  342.2 24.7 %copy.8 = bf16[1536,6144]{1,0:T(8,128)(2,1)} copy(bf16[1536,6144]{0,1:T(8,128)(2,1)} %fusion) | data formatting | bytes 37748736
  366.9 16.0 %convolution_convert_fusion = bf16[6144,1536]{1,0:T(8,128)(2,1)} fusion(bf16[512,6144]{1,0:T(8,128)(2,1)} %all-gather.7.cloned.1.call-done, bf16[512,1536]{1,0:T(8,128)(2,1)S(1)} %copy-done), kind=kOutput, calls=%fused_computation | convolution fusion | flops 9673113600 | bytes 26738688 | tf_op jit(solution)/shard_map/dot_general | solution.py:25
  382.9 2.0 reduce-scatter.11.cloned.1.call-done
  (4 shorter events, 0.0 us)
Async XLA Ops:
  7.2 42.2 %all-gather.9.cloned.1.call-start = ((), (), s32[]{:S(2)}) async-start(), calls=%async_computation.8 | async-start | bytes 1966080 | tf_op jit(solution)/shard_map/all_gather | solution.py:31
  7.9 79.1 %all-gather.5.cloned.1.call-start = ((), (), s32[]{:S(2)}) async-start(), calls=%async_computation.4 | async-start | bytes 1966080 | tf_op jit(solution)/shard_map/all_gather | solution.py:31
  8.6 138.7 %reduce-scatter.9.cloned.1.call-start = ((), (), s32[]{:S(2)}) async-start(), calls=%async_computation.9 | async-start | bytes 7864320 | tf_op jit(solution)/shard_map/reduce_scatter | solution.py:41
  65.3 143.5 %reduce-scatter.5.cloned.1.call-start = ((), (), s32[]{:S(2)}) async-start(), calls=%async_computation.5 | async-start | bytes 7864320 | tf_op jit(solution)/shard_map/reduce_scatter | solution.py:41
  102.8 158.3 %all-gather.7.cloned.1.call-start = ((), (), s32[]{:S(2)}) async-start(), calls=%async_computation.6 | async-start | bytes 7864320 | tf_op jit(solution)/shard_map/all_gather | solution.py:49
  214.6 94.9 %all-gather.11.cloned.1.call-start = ((), (), s32[]{:S(2)}) async-start(), calls=%async_computation.10 | async-start | bytes 7864320 | tf_op jit(solution)/shard_map/all_gather | solution.py:49
  215.2 167.7 %reduce-scatter.7.cloned.1.call-start = ((), (), s32[]{:S(2)}) async-start(), calls=%async_computation.7 | async-start | bytes 1966080 | tf_op jit(solution)/shard_map/reduce_scatter | solution.py:35
  277.8 48.4 %copy-start.1 = (bf16[512,1536]{1,0:T(8,128)(2,1)S(1)}, bf16[512,1536]{1,0:T(8,128)(2,1)}, u32[]{:S(2)}) copy-start(bf16[512,1536]{1,0:T(8,128)(2,1)} %all-gather.5.cloned.1.call-done) | copy-start | bytes 4718596
  277.8 107.1 %reduce-scatter.11.cloned.1.call-start = ((), (), s32[]{:S(2)}) async-start(), calls=%async_computation.11 | async-start | bytes 1966080 | tf_op jit(solution)/shard_map/reduce_scatter | solution.py:35
  342.2 24.7 %copy-start = (bf16[512,1536]{1,0:T(8,128)(2,1)S(1)}, bf16[512,1536]{1,0:T(8,128)(2,1)}, u32[]{:S(2)}) copy-start(bf16[512,1536]{1,0:T(8,128)(2,1)} %all-gather.9.cloned.1.call-done) | copy-start | bytes 4718596
Sparse Core Ops, SparseCore 0:
  9.6 39.7 all-gather.8
  51.0 35.9 all-gather.4
  90.1 57.2 reduce-scatter.8
  150.5 58.3 reduce-scatter.4
  214.7 46.3 all-gather.6
  263.1 46.3 all-gather.10
  312.4 35.2 reduce-scatter.6
  350.6 34.2 reduce-scatter.10
where the time goes:
time: 393 us; the launch traced here: 392 us
  waiting for transfers between devices  250 us (64%)
  matrix products  97 us (25%)
  local copies, waits for them, and re-layouts  24.7 us (6%)
  between operations  14.2 us (4%)
  other arithmetic  5.68 us (1%)
    reduce_scatter x2, waiting for transfers between devices, hidden_sum(): lax.psum_scatter(product(left_mat, right_mat, flipped).astype(jnp.bfloat1...  106 us
    all_gather x2, waiting for transfers between devices, hidden_gather(): return lax.all_gather(share_part, 'gx', axis=1, tiled=True)  77.4 us
    all_gather x2, waiting for transfers between devices, token_gather(): return lax.all_gather(local_rows, 'gy', axis=0, tiled=True)  62.3 us
    dot_general x2, matrix products, product(): lax.dot_general(left_mat, right_mat, (((1,), (1,)), ((), ())), preferred_...  32.5 us
    dot_general x2, matrix products, product(): return jnp.dot(left_mat, right_mat, preferred_element_type=jnp.float32)  32.5 us
    dot_general x2, matrix products, inner_rows(): lax.dot_general(left_mat, right_mat, (((0,), (0,)), ((), ())), preferred_...  32 us
    unnamed x5, local copies, waits for them, and re-layouts  24.7 us
  transfers between devices with their start and end apart: 8, of which 7 were waited for; matrix products, arithmetic and copies ran while one was open for 31% of the time, Pallas kernels for 0%

commit v1 on v0

--- a/solution.py
+++ b/solution.py
@@ -27,15 +27,12 @@
     )
 
 
-def token_gather(local_rows):
-    return lax.all_gather(local_rows, "gy", axis=0, tiled=True)
+def general_shards(tokens, w_in, w_out, grad_out):
+    def token_gather(local_rows):
+        return lax.all_gather(local_rows, "gy", axis=0, tiled=True)
 
-
-def token_total(term):
-    return lax.psum_scatter(term.astype(jnp.bfloat16), "gy", scatter_dimension=0, tiled=True)
-
-
-def shards(tokens, w_in, w_out, grad_out):
+    def token_total(term):
+        return lax.psum_scatter(term.astype(jnp.bfloat16), "gy", scatter_dimension=0, tiled=True)
 
     def hidden_sum(left_mat, right_mat, flipped):
         return lax.psum_scatter(
@@ -63,6 +60,112 @@
     return (output, grad_tokens, grad_w_in, grad_w_out)
 
 
+CHUNKS = 4
+SPLIT_CHUNKS = 2
+DEPTH = 3
+
+
+def after(value, earlier):
+    return lax.optimization_barrier((value, earlier))
+
+
+def square_shards(n_gy, tokens, w_in, w_out, grad_out):
+    bf16, f32 = jnp.bfloat16, jnp.float32
+    width = w_in.shape[1] // CHUNKS
+    half = width // 2
+    rows = tokens.shape[0]
+    is_first = lax.axis_index("gx") % 2 == 0
+    forward = [(i, (i + 1) % n_gy) for i in range(n_gy)]
+    backward = [(i, (i + n_gy - 1) % n_gy) for i in range(n_gy)]
+    sibling = [(i, i ^ 1) for i in range(4)]
+    across = [(i, i ^ 2) for i in range(4)]
+
+    def ring_gather(block):
+        blocks = [block]
+        for _ in range(n_gy - 1):
+            blocks.append(lax.ppermute(blocks[-1], "gy", forward))
+        return blocks
+
+    crossed = []
+
+    def full_sum(left_mat, right_mat, flipped):
+        if len(crossed) >= DEPTH:
+            left_mat, crossed[-DEPTH][1] = after(left_mat, crossed[-DEPTH][1])
+        partial = product(left_mat, right_mat, flipped).astype(bf16)
+        first, second = partial[:, :half], partial[:, half:]
+        kept = jnp.where(is_first, first, second).astype(f32)
+        given = jnp.where(is_first, second, first)
+        mine = (kept + lax.ppermute(given, "gx", sibling).astype(f32)).astype(bf16)
+        crossed.append([mine, lax.ppermute(mine, "gx", across)])
+        return crossed[-1]
+
+    def added(pair):
+        return pair[0].astype(f32) + pair[1].astype(f32)
+
+    def share(part):
+        other = lax.ppermute(part, "gx", sibling)
+        return jnp.concatenate(
+            [jnp.where(is_first, part, other), jnp.where(is_first, other, part)], axis=1
+        )
+
+    def ring_total(term, beside=None):
+        parts = [term[r * rows : (r + 1) * rows].astype(bf16).astype(f32) for r in range(n_gy)]
+        moving = parts[n_gy - 1]
+        for r in range(n_gy - 2, -1, -1):
+            if beside is not None and r == n_gy - 3:
+                parts[r], beside = after(parts[r], beside)
+            moving = lax.ppermute(moving.astype(bf16), "gy", backward).astype(f32) + parts[r]
+        return moving.astype(bf16), beside
+
+    token_blocks = ring_gather(tokens)
+    grad_start, token_blocks[1] = after(grad_out, token_blocks[1])
+    grad_blocks = ring_gather(grad_start)
+    n_half = n_gy // 2
+    near = jnp.concatenate(token_blocks[:n_half])
+    far = jnp.concatenate(token_blocks[n_half:])
+    token_rows = jnp.concatenate([near, far])
+    grad_rows = jnp.concatenate(grad_blocks)
+
+    def columns(c):
+        return w_in[:, c * width : (c + 1) * width]
+
+    def activated(pairs):
+        pre = jnp.concatenate([added(p) for p in pairs])
+        return pre, share(jax.nn.gelu(pre, approximate=True).astype(bf16))
+
+    def grad_pair(c):
+        return full_sum(grad_rows, w_out[c * width : (c + 1) * width, :], True)
+
+    pairs = [[full_sum(near, columns(c), False)] for c in range(SPLIT_CHUNKS)]
+    for c in range(SPLIT_CHUNKS):
+        pairs[c].append(full_sum(far, columns(c), False))
+    for c in range(SPLIT_CHUNKS, CHUNKS):
+        pairs.append([full_sum(token_rows, columns(c), False)])
+    grad_pairs = [grad_pair(0), grad_pair(1)]
+    pre, hidden = zip(*[activated(p) for p in pairs])
+    hidden_all = jnp.concatenate(hidden, axis=1)
+
+    out_term = product(hidden_all, w_out, False).astype(bf16)
+    grad_pairs.append(grad_pair(2))
+    grad_rows, out_term = after(grad_rows, out_term)
+    output, _ = ring_total(out_term)
+    grad_pairs.append(grad_pair(3))
+    grad_pre, grad_term = [], 0.0
+
+    def grad_chunk(c):
+        return share((added(grad_pairs[c]) * gelu_slope(pre[c])).astype(bf16))
+
+    hidden_all, grad_pairs[3][0] = after(hidden_all, grad_pairs[3][0])
+    grad_w_out = inner_rows(hidden_all, grad_rows).astype(bf16)
+    grad_pairs[2][1], grad_w_out = after(grad_pairs[2][1], grad_w_out)
+    for c in range(CHUNKS):
+        grad_pre.append(grad_chunk(c))
+        grad_term = grad_term + product(grad_pre[c], columns(c), True)
+    grad_w_in = inner_rows(token_rows, jnp.concatenate(grad_pre, axis=1)).astype(bf16)
+    grad_tokens, grad_w_in = ring_total(grad_term, grad_w_in)
+    return (output, grad_tokens, grad_w_in, grad_w_out)
+
+
 def solution(mesh):
     in_specs = (P(("groups", "gy"), "gx"), P("gx", "gy"), P("gy", "gx"), P(("groups", "gy"), "gx"))
     out_specs = (
@@ -71,4 +174,9 @@
         P(("groups", "gx"), "gy"),
         P(("groups", "gy"), "gx"),
     )
+    n_gy = mesh.shape["gy"]
+    if mesh.shape["gx"] == 4 and n_gy % 2 == 0:
+        shards = lambda *arrays: square_shards(n_gy, *arrays)
+    else:
+        shards = general_shards
     return jax.shard_map(shards, mesh=mesh, in_specs=in_specs, out_specs=out_specs, check_vma=False)

time: 393 us -> 297 us (0.76); the launches traced: 392 us -> 291 us
  waiting for transfers between devices: 250 us -> 130 us
  starting transfers between devices: 0.5 us -> 30.2 us
  local copies, waits for them, and re-layouts: 24.7 us -> 1.41 us
  other arithmetic: 5.68 us -> 20.3 us
  between operations: 14.2 us -> 1.86 us
  matrix products: 97 us -> 108 us
    all_gather x4 -> x0, waiting for transfers between devices: 140 us -> none  [the longest x2 77.4 us: hidden_gather(): return lax.all_gather(share_part, 'gx', axis=1, tiled=True)]
    ppermute x0 -> x40, waiting for transfers between devices: none -> 130 us  [the longest x10 54.6 us: full_sum(): crossed.append([mine, lax.ppermute(mine, 'gx', across)])]
    reduce_scatter x4 -> x0, waiting for transfers between devices: 108 us -> none  [the longest x2 106 us: hidden_sum(): lax.psum_scatter(product(left_mat, right_mat, flipped).astype(jnp.bfloat1...]
    ppermute x0 -> x40, starting transfers between devices: none -> 30.2 us  [the longest x10 10.8 us: full_sum(): crossed.append([mine, lax.ppermute(mine, 'gx', across)])]
    unnamed x5 -> x19, local copies, waits for them, and re-layouts: 24.7 us -> 1.25 us
    convert_element_type x1 -> x23, other arithmetic: 5.68 us -> 15.1 us  [the longest x4 7.84 us: grad_chunk(): return share((added(grad_pairs[c]) * gelu_slope(pre[c])).astype(bf16))]
    dot_general x2 -> x8, matrix products: 32.5 us -> 40.7 us  [product(): lax.dot_general(left_mat, right_mat, (((1,), (1,)), ((), ())), preferred_...]
    dot_general x2 -> x7, matrix products: 32.5 us -> 34.8 us  [product(): return jnp.dot(left_mat, right_mat, preferred_element_type=jnp.float32)]
  transfers between devices with their start and end apart: 8 -> 40, of which waited for: 7 -> 13; matrix products, arithmetic and copies ran while one was open for 31% -> 41% of each run, Pallas kernels for 0% -> 0%
where the time goes in v1:
time: 297 us; the launch traced here: 291 us
  waiting for transfers between devices  130 us (44%)
  matrix products  108 us (36%)
  starting transfers between devices  30.2 us (10%)
  other arithmetic  20.3 us (7%)
    ppermute x10, waiting for transfers between devices, full_sum(): crossed.append([mine, lax.ppermute(mine, 'gx', across)])  54.6 us
    ppermute x6, waiting for transfers between devices, ring_gather(): blocks.append(lax.ppermute(blocks[-1], 'gy', forward))  53.7 us
    dot_general x8, matrix products, product(): lax.dot_general(left_mat, right_mat, (((1,), (1,)), ((), ())), preferred_...  40.7 us
    dot_general x7, matrix products, product(): return jnp.dot(left_mat, right_mat, preferred_element_type=jnp.float32)  34.8 us
    dot_general x2, matrix products, inner_rows(): lax.dot_general(left_mat, right_mat, (((0,), (0,)), ((), ())), preferred_...  32.5 us
    ppermute x6, waiting for transfers between devices, ring_total(): lax.ppermute(moving.astype(bf16), 'gy', backward).astype(f32) + parts[r]  21.1 us
    ppermute x10, starting transfers between devices, full_sum(): crossed.append([mine, lax.ppermute(mine, 'gx', across)])  10.8 us
    ppermute x6, starting transfers between devices, ring_total(): lax.ppermute(moving.astype(bf16), 'gy', backward).astype(f32) + parts[r]  10.1 us
  transfers between devices with their start and end apart: 40, of which 13 were waited for; matrix products, arithmetic and copies ran while one was open for 41% of the time, Pallas kernels for 0%

profile of v1, /device:TPU:0, one launch (start us, length us, event | category | flops | bytes accessed | tf_op | source)
XLA Modules:
  0.0 291.4 jit_solution(1397757008474252303)
XLA Ops:
  0.6 3.1 %collective-permute-start = (bf16[128,1536]{1,0:T(8,128)(2,1)}, bf16[128,1536]{1,0:T(8,128)(2,1)S(1)}, u32[]{:S(2)}, u32[]{:S(2)}) collective-permute-start(bf16[128,1536]{1,0:T(8,128)(2,1)} %param.4), channel_id=1, source_target_pairs={{0,1},{1,2},{2,3},{3,0},{4,5},{5,6},{6,7},{7,4},{8,9},{9,10},{10,1... | collective-permute-start | bytes 1179656 | tf_op jit(solution)/shard_map/ppermute | solution.py:86
  4.8 10.3 %collective-permute-done = bf16[128,1536]{1,0:T(8,128)(2,1)S(1)} collective-permute-done((bf16[128,1536]{1,0:T(8,128)(2,1)}, bf16[128,1536]{1,0:T(8,128)(2,1)S(1)}, u32[]{:S(2)}, u32[]{:S(2)}) %collective-permute-start) | collective-permute-done | bytes 393248 | tf_op jit(solution)/shard_map/ppermute | solution.py:86
  15.1 3.9 %fusion.64 = bf16[256,1536]{1,0:T(8,128)(2,1)S(1)} fusion(bf16[256,1536]{1,0:T(8,128)(2,1)S(1)} %get-tuple-element.70, bf16[1536,6144]{1,0:T(8,128)(2,1)} %param.5), kind=kOutput, calls=%fused_computation.43 | convolution fusion | flops 1208352768 | bytes 6291456 | tf_op jit(solution)/shard_map/dot_general | solution.py:21
  19.0 4.5 %fusion.58 = bf16[256,1536]{1,0:T(8,128)(2,1)S(1)} fusion(bf16[256,1536]{1,0:T(8,128)(2,1)S(1)} %get-tuple-element.70, bf16[1536,6144]{1,0:T(8,128)(2,1)} %param.5), kind=kOutput, calls=%fused_computation.41 | convolution fusion | flops 1208352768 | bytes 6291456 | tf_op jit(solution)/shard_map/dot_general | solution.py:21
  28.1 9.3 %collective-permute-done.1 = bf16[128,1536]{1,0:T(8,128)(2,1)S(1)} collective-permute-done((bf16[128,1536]{1,0:T(8,128)(2,1)S(1)}, bf16[128,1536]{1,0:T(8,128)(2,1)S(1)}, u32[]{:S(2)}, u32[]{:S(2)}) %collective-permute-start.1) | collective-permute-done | bytes 393248 | tf_op jit(solution)/shard_map/ppermute | solution.py:86
  37.4 8.4 %collective-permute-done.5 = bf16[128,1536]{1,0:T(8,128)(2,1)S(1)} collective-permute-done((bf16[128,1536]{1,0:T(8,128)(2,1)S(1)}, bf16[128,1536]{1,0:T(8,128)(2,1)S(1)}, u32[]{:S(2)}, u32[]{:S(2)}) %collective-permute-start.5) | collective-permute-done | bytes 393248 | tf_op jit(solution)/shard_map/ppermute | solution.py:86
  45.9 15.0 %collective-permute-done.6 = bf16[128,1536]{1,0:T(8,128)(2,1)S(1)} collective-permute-done((bf16[128,1536]{1,0:T(8,128)(2,1)S(1)}, bf16[128,1536]{1,0:T(8,128)(2,1)S(1)}, u32[]{:S(2)}, u32[]{:S(2)}) %collective-permute-start.6) | collective-permute-done | bytes 393248 | tf_op jit(solution)/shard_map/ppermute | solution.py:86
  64.5 2.6 fusion.40
  70.6 10.7 %collective-permute-done.3 = bf16[128,1536]{1,0:T(8,128)(2,1)S(1)} collective-permute-done((bf16[128,1536]{1,0:T(8,128)(2,1)S(1)}, bf16[128,1536]{1,0:T(8,128)(2,1)S(1)}, u32[]{:S(2)}, u32[]{:S(2)}) %collective-permute-start.3) | collective-permute-done | bytes 393248 | tf_op jit(solution)/shard_map/ppermute | solution.py:86
  81.4 6.9 %collective-permute-done.14 = bf16[256,768]{1,0:T(8,128)(2,1)S(1)} collective-permute-done((bf16[256,768]{1,0:T(8,128)(2,1)S(1)}, bf16[256,768]{1,0:T(8,128)(2,1)S(1)}, u32[]{:S(2)}, u32[]{:S(2)}) %collective-permute-start.14) | collective-permute-done | bytes 393248 | tf_op jit(solution)/shard_map/ppermute | solution.py:99
  88.8 5.0 %fusion.46 = bf16[512,1536]{1,0:T(8,128)(2,1)S(1)} fusion(bf16[512,1536]{1,0:T(8,128)(2,1)S(1)} %constant_dynamic-update-slice_fusion, bf16[6144,1536]{1,0:T(8,128)(2,1)} %param.6), kind=kOutput, calls=%fused_computation.36 | convolution fusion | flops 2416705536 | bytes 7864320 | tf_op jit(solution)/shard_map/dot_general | solution.py:18
  96.1 5.0 %fusion.43 = bf16[512,1536]{1,0:T(8,128)(2,1)S(1)} fusion(bf16[512,1536]{1,0:T(8,128)(2,1)S(1)} %get-tuple-element.36, bf16[1536,6144]{1,0:T(8,128)(2,1)} %param.5), kind=kOutput, calls=%fused_computation.35 | convolution fusion | flops 2416705536 | bytes 7864320 | tf_op jit(solution)/shard_map/dot_general | solution.py:21
  102.4 12.8 %collective-permute-done.17 = bf16[512,768]{1,0:T(8,128)(2,1)S(1)} collective-permute-done((bf16[512,768]{1,0:T(8,128)(2,1)S(1)}, bf16[512,768]{1,0:T(8,128)(2,1)S(1)}, u32[]{:S(2)}, u32[]{:S(2)}) %collective-permute-start.17) | collective-permute-done | bytes 786464 | tf_op jit(solution)/shard_map/ppermute | solution.py:99
  115.2 5.0 %fusion.49 = bf16[512,1536]{1,0:T(8,128)(2,1)S(1)} fusion(bf16[512,1536]{1,0:T(8,128)(2,1)S(1)} %constant_dynamic-update-slice_fusion, bf16[6144,1536]{1,0:T(8,128)(2,1)} %param.6), kind=kOutput, calls=%fused_computation.37 | convolution fusion | flops 2416705536 | bytes 7864320 | tf_op jit(solution)/shard_map/dot_general | solution.py:18
  124.7 24.2 %collective-permute-done.20 = bf16[512,768]{1,0:T(8,128)(2,1)S(1)} collective-permute-done((bf16[512,768]{1,0:T(8,128)(2,1)S(1)}, bf16[512,768]{1,0:T(8,128)(2,1)S(1)}, u32[]{:S(2)}, u32[]{:S(2)}) %collective-permute-start.20) | collective-permute-done | bytes 786464 | tf_op jit(solution)/shard_map/ppermute | solution.py:99
  148.9 5.0 %fusion.52 = bf16[512,1536]{1,0:T(8,128)(2,1)S(1)} fusion(bf16[512,1536]{1,0:T(8,128)(2,1)S(1)} %constant_dynamic-update-slice_fusion, bf16[6144,1536]{1,0:T(8,128)(2,1)} %param.6), kind=kOutput, calls=%fused_computation.38 | convolution fusion | flops 2416705536 | bytes 7864320 | tf_op jit(solution)/shard_map/dot_general | solution.py:18
  154.1 10.7 %collective-permute-done.29 = bf16[512,768]{1,0:T(8,128)(2,1)S(1)} collective-permute-done((bf16[512,768]{1,0:T(8,128)(2,1)S(1)}, bf16[512,768]{1,0:T(8,128)(2,1)S(1)}, u32[]{:S(2)}, u32[]{:S(2)}) %collective-permute-start.29) | collective-permute-done | bytes 786464 | tf_op jit(solution)/shard_map/ppermute | solution.py:99
  171.5 16.1 %convolution_convert_fusion.2 = bf16[512,1536]{1,0:T(8,128)(2,1)S(1)} fusion(bf16[512,6144]{1,0:T(8,128)(2,1)S(1)} %select_dynamic-update-slice_fusion, bf16[6144,1536]{1,0:T(8,128)(2,1)} %param.6), kind=kOutput, calls=%fused_computation.40 | convolution fusion | flops 9664462848 | bytes 26738688 | tf_op jit(solution)/shard_map/dot_general | solution.py:21
  187.7 3.6 %collective-permute-start.22 = (bf16[128,1536]{1,0:T(8,128)(2,1)S(1)}, bf16[128,1536]{1,0:T(8,128)(2,1)S(1)}, u32[]{:S(2)}, u32[]{:S(2)}) collective-permute-start(bf16[128,1536]{1,0:T(8,128)(2,1)S(1)} %slice.134), channel_id=1, source_target_pairs={{0,3},{1,0},{2,1},{3,2},{4,7},{5,4},{6,5},{7,6},{8,11},{9,8},{10,9... | collective-permute-start | bytes 1179656 | tf_op jit(solution)/shard_map/ppermute | solution.py:117
  191.3 5.0 %fusion.55 = bf16[512,1536]{1,0:T(8,128)(2,1)S(1)} fusion(bf16[512,1536]{1,0:T(8,128)(2,1)S(1)} %constant_dynamic-update-slice_fusion, bf16[6144,1536]{1,0:T(8,128)(2,1)} %param.6), kind=kOutput, calls=%fused_computation.39 | convolution fusion | flops 2416705536 | bytes 7864320 | tf_op jit(solution)/shard_map/dot_general | solution.py:18
  200.1 4.3 %collective-permute-start.23 = (bf16[128,1536]{1,0:T(8,128)(2,1)S(1)}, bf16[128,1536]{1,0:T(8,128)(2,1)}, u32[]{:S(2)}, u32[]{:S(2)}) collective-permute-start(bf16[128,1536]{1,0:T(8,128)(2,1)S(1)} %add_convert_fusion.11), channel_id=1, source_target_pairs={{0,3},{1,0},{2,1},{3,2},{4,7},{5,4},{6,5},{7,6},{8,11},{9,8},{10,9... | collective-permute-start | bytes 1179656 | tf_op jit(solution)/shard_map/ppermute | solution.py:117
  205.6 16.5 %convolution_convert_fusion.1 = bf16[6144,1536]{1,0:T(8,128)(2,1)} fusion(bf16[512,6144]{1,0:T(8,128)(2,1)} %copy-done.4, bf16[512,1536]{1,0:T(8,128)(2,1)} %copy-done.1), kind=kOutput, calls=%fused_computation.1 | convolution fusion | flops 9673113600 | bytes 26738688 | tf_op jit(solution)/shard_map/dot_general | solution.py:25
  222.2 2.4 fusion.122
  225.6 4.5 %fusion.16 = f32[512,1536]{1,0:T(8,128)S(1)} fusion(bf16[1536,6144]{1,0:T(8,128)(2,1)} %param.5, bf16[512,768]{1,0:T(8,128)(2,1)S(1)} %get-tuple-element.59, bf16[512,768]{1,0:T(8,128)(2,1)S(1)} %get-tuple-element.61), kind=kOutput, calls=%fused_computation.18 | convolution fusion | flops 2419064832 | bytes 9437184 | tf_op jit(solution)/shard_map/dot_general | solution.py:18
  230.2 2.4 fusion.129
  233.6 4.5 %fusion.12 = f32[512,1536]{1,0:T(8,128)S(1)} fusion(bf16[1536,6144]{1,0:T(8,128)(2,1)} %param.5, bf16[512,768]{1,0:T(8,128)(2,1)S(1)} %get-tuple-element.55, bf16[512,768]{1,0:T(8,128)(2,1)S(1)} %get-tuple-element.57), kind=kOutput, calls=%fused_computation.14 | convolution fusion | flops 2419064832 | bytes 9437184 | tf_op jit(solution)/shard_map/dot_general | solution.py:18
  238.7 6.6 %fusion.8 = f32[512,1536]{1,0:T(8,128)S(1)} fusion(bf16[1536,6144]{1,0:T(8,128)(2,1)} %param.5, bf16[512,768]{1,0:T(8,128)(2,1)S(1)} %get-tuple-element.51, bf16[512,768]{1,0:T(8,128)(2,1)S(1)} %get-tuple-element.53), kind=kOutput, calls=%fused_computation.10 | convolution fusion | flops 2419064832 | bytes 9437184 | tf_op jit(solution)/shard_map/dot_general | solution.py:18
  245.3 5.1 %fusion.37 = bf16[512,1536]{1,0:T(8,128)(2,1)S(1)} fusion(f32[512,1536]{1,0:T(8,128)S(1)} %fusion.8, f32[512,1536]{1,0:T(8,128)S(1)} %fusion.12, f32[512,1536]{1,0:T(8,128)S(1)} %fusion.16, bf16[1536,6144]{1,0:T(8,128)(2,1)} %param.5, bf16[512,768]{1,0:T(8,128)(2,1)S(1)} %get-tuple-element.63, bf16[512,768]{1,0:T(8,128)(2,1)S(1)} %get-tuple-element.65), kind=kOutput, calls=%fused_computation.33 | convolution fusion | flops 2422210560 | bytes 17301504 | tf_op jit(solution)/shard_map/dot_general | solution.py:18
  251.8 10.7 %collective-permute-done.37 = bf16[128,1536]{1,0:T(8,128)(2,1)S(1)} collective-permute-done((bf16[128,1536]{1,0:T(8,128)(2,1)S(1)}, bf16[128,1536]{1,0:T(8,128)(2,1)S(1)}, u32[]{:S(2)}, u32[]{:S(2)}) %collective-permute-start.37) | collective-permute-done | bytes 393248 | tf_op jit(solution)/shard_map/ppermute | solution.py:117
  262.6 1.8 collective-permute-start.38
  264.4 16.0 %convolution_convert_fusion = bf16[1536,6144]{1,0:T(8,128)(2,1)} fusion(bf16[512,1536]{1,0:T(8,128)(2,1)S(1)} %copy-done.3, bf16[512,6144]{1,0:T(8,128)(2,1)} %copy-done.5), kind=kOutput, calls=%fused_computation | convolution fusion | flops 9673113600 | bytes 26738688 | tf_op jit(solution)/shard_map/dot_general | solution.py:25
  281.5 8.6 %collective-permute-done.39 = bf16[128,1536]{1,0:T(8,128)(2,1)S(1)} collective-permute-done((bf16[128,1536]{1,0:T(8,128)(2,1)S(1)}, bf16[128,1536]{1,0:T(8,128)(2,1)S(1)}, u32[]{:S(2)}, u32[]{:S(2)}) %collective-permute-start.39) | collective-permute-done | bytes 393248 | tf_op jit(solution)/shard_map/ppermute | solution.py:117
  (142 shorter events, 38.9 us)
Async XLA Ops:
  0.6 14.4 %collective-permute-start = (bf16[128,1536]{1,0:T(8,128)(2,1)}, bf16[128,1536]{1,0:T(8,128)(2,1)S(1)}, u32[]{:S(2)}, u32[]{:S(2)}) collective-permute-start(bf16[128,1536]{1,0:T(8,128)(2,1)} %param.4), channel_id=1, source_target_pairs={{0,1},{1,2},{2,3},{3,0},{4,5},{5,6},{6,7},{7,4},{8,9},{9,10},{10,1... | collective-permute-start | bytes 1179656 | tf_op jit(solution)/shard_map/ppermute | solution.py:86
  23.5 13.9 %collective-permute-start.1 = (bf16[128,1536]{1,0:T(8,128)(2,1)S(1)}, bf16[128,1536]{1,0:T(8,128)(2,1)S(1)}, u32[]{:S(2)}, u32[]{:S(2)}) collective-permute-start(bf16[128,1536]{1,0:T(8,128)(2,1)S(1)} %copy-done), channel_id=1, source_target_pairs={{0,1},{1,2},{2,3},{3,0},{4,5},{5,6},{6,7},{7,4},{8,9},{9,10},{10,1... | collective-permute-start | bytes 1179656 | tf_op jit(solution)/shard_map/ppermute | solution.py:86
  24.3 21.5 %collective-permute-start.5 = (bf16[128,1536]{1,0:T(8,128)(2,1)S(1)}, bf16[128,1536]{1,0:T(8,128)(2,1)S(1)}, u32[]{:S(2)}, u32[]{:S(2)}) collective-permute-start(bf16[128,1536]{1,0:T(8,128)(2,1)S(1)} %collective-permute-done), channel_id=1, source_target_pairs={{0,1},{1,2},{2,3},{3,0},{4,5},{5,6},{6,7},{7,4},{8,9},{9,10},{10,1... | collective-permute-start | bytes 1179656 | tf_op jit(solution)/shard_map/ppermute | solution.py:86
  25.8 36.8 %collective-permute-start.12 = (bf16[256,768]{1,0:T(8,128)(2,1)S(1)}, bf16[256,768]{1,0:T(8,128)(2,1)S(1)}, u32[]{:S(2)}, u32[]{:S(2)}) collective-permute-start(bf16[256,768]{1,0:T(8,128)(2,1)S(1)} %add_convert_fusion.13), channel_id=1, source_target_pairs={{0,8},{4,12},{8,0},{12,4},{1,9},{5,13},{9,1},{13,5},{2,10},{6,14},... | collective-permute-start | bytes 1179656 | tf_op jit(solution)/shard_map/ppermute | solution.py:99
  27.5 35.1 %collective-permute-start.7 = (bf16[256,768]{1,0:T(8,128)(2,1)S(1)}, bf16[256,768]{1,0:T(8,128)(2,1)S(1)}, u32[]{:S(2)}, u32[]{:S(2)}) collective-permute-start(bf16[256,768]{1,0:T(8,128)(2,1)S(1)} %add_convert_fusion.15), channel_id=1, source_target_pairs={{0,8},{4,12},{8,0},{12,4},{1,9},{5,13},{9,1},{13,5},{2,10},{6,14},... | collective-permute-start | bytes 1179656 | tf_op jit(solution)/shard_map/ppermute | solution.py:99
  37.4 30.0 %collective-permute-start.2 = (bf16[128,1536]{1,0:T(8,128)(2,1)S(1)}, bf16[128,1536]{1,0:T(8,128)(2,1)S(1)}, u32[]{:S(2)}, u32[]{:S(2)}) collective-permute-start(bf16[128,1536]{1,0:T(8,128)(2,1)S(1)} %collective-permute-done.1), channel_id=1, source_target_pairs={{0,1},{1,2},{2,3},{3,0},{4,5},{5,6},{6,7},{7,4},{8,9},{9,10},{10,1... | collective-permute-start | bytes 1179656 | tf_op jit(solution)/shard_map/ppermute | solution.py:86
  45.8 15.1 %collective-permute-start.6 = (bf16[128,1536]{1,0:T(8,128)(2,1)S(1)}, bf16[128,1536]{1,0:T(8,128)(2,1)S(1)}, u32[]{:S(2)}, u32[]{:S(2)}) collective-permute-start(bf16[128,1536]{1,0:T(8,128)(2,1)S(1)} %collective-permute-done.5), channel_id=1, source_target_pairs={{0,1},{1,2},{2,3},{3,0},{4,5},{5,6},{6,7},{7,4},{8,9},{9,10},{10,1... | collective-permute-start | bytes 1179656 | tf_op jit(solution)/shard_map/ppermute | solution.py:86
  67.2 27.2 %collective-permute-start.16 = (bf16[512,768]{1,0:T(8,128)(2,1)S(1)}, bf16[512,768]{1,0:T(8,128)(2,1)S(1)}, u32[]{:S(2)}, u32[]{:S(2)}) collective-permute-start(bf16[512,768]{1,0:T(8,128)(2,1)S(1)} %broadcast_select_fusion.13), channel_id=1, source_target_pairs={{0,4},{4,0},{8,12},{12,8},{1,5},{5,1},{9,13},{13,9},{2,6},{6,2},{1... | collective-permute-start | bytes 2359304 | tf_op jit(solution)/shard_map/ppermute | solution.py:98
  67.4 13.8 %collective-permute-start.3 = (bf16[128,1536]{1,0:T(8,128)(2,1)S(1)}, bf16[128,1536]{1,0:T(8,128)(2,1)S(1)}, u32[]{:S(2)}, u32[]{:S(2)}) collective-permute-start(bf16[128,1536]{1,0:T(8,128)(2,1)S(1)} %collective-permute-done.2), channel_id=1, source_target_pairs={{0,1},{1,2},{2,3},{3,0},{4,5},{5,6},{6,7},{7,4},{8,9},{9,10},{10,1... | collective-permute-start | bytes 1179656 | tf_op jit(solution)/shard_map/ppermute | solution.py:86
  68.2 13.0 %collective-permute-start.9 = (bf16[256,768]{1,0:T(8,128)(2,1)S(1)}, bf16[256,768]{1,0:T(8,128)(2,1)S(1)}, u32[]{:S(2)}, u32[]{:S(2)}) collective-permute-start(bf16[256,768]{1,0:T(8,128)(2,1)S(1)} %add_convert_fusion.14), channel_id=1, source_target_pairs={{0,8},{4,12},{8,0},{12,4},{1,9},{5,13},{9,1},{13,5},{2,10},{6,14},... | collective-permute-start | bytes 1179656 | tf_op jit(solution)/shard_map/ppermute | solution.py:99
  69.7 18.5 %collective-permute-start.14 = (bf16[256,768]{1,0:T(8,128)(2,1)S(1)}, bf16[256,768]{1,0:T(8,128)(2,1)S(1)}, u32[]{:S(2)}, u32[]{:S(2)}) collective-permute-start(bf16[256,768]{1,0:T(8,128)(2,1)S(1)} %add_convert_fusion.12), channel_id=1, source_target_pairs={{0,8},{4,12},{8,0},{12,4},{1,9},{5,13},{9,1},{13,5},{2,10},{6,14},... | collective-permute-start | bytes 1179656 | tf_op jit(solution)/shard_map/ppermute | solution.py:99
  88.7 34.2 %collective-permute-start.10 = (bf16[512,768]{1,0:T(8,128)(2,1)S(1)}, bf16[512,768]{1,0:T(8,128)(2,1)S(1)}, u32[]{:S(2)}, u32[]{:S(2)}) collective-permute-start(bf16[512,768]{1,0:T(8,128)(2,1)S(1)} %fusion.77), channel_id=1, source_target_pairs={{0,4},{4,0},{8,12},{12,8},{1,5},{5,1},{9,13},{13,9},{2,6},{6,2},{1... | collective-permute-start | bytes 2359304 | tf_op jit(solution)/shard_map/ppermute | solution.py:106
  93.9 7.4 %collective-permute-start.25 = (bf16[512,768]{1,0:T(8,128)(2,1)S(1)}, bf16[512,768]{1,0:T(8,128)(2,1)S(1)}, u32[]{:S(2)}, u32[]{:S(2)}) collective-permute-start(bf16[512,768]{1,0:T(8,128)(2,1)S(1)} %broadcast_select_fusion.11), channel_id=1, source_target_pairs={{0,4},{4,0},{8,12},{12,8},{1,5},{5,1},{9,13},{13,9},{2,6},{6,2},{1... | collective-permute-start | bytes 2359304 | tf_op jit(solution)/shard_map/ppermute | solution.py:98
  94.8 20.5 %collective-permute-start.17 = (bf16[512,768]{1,0:T(8,128)(2,1)S(1)}, bf16[512,768]{1,0:T(8,128)(2,1)S(1)}, u32[]{:S(2)}, u32[]{:S(2)}) collective-permute-start(bf16[512,768]{1,0:T(8,128)(2,1)S(1)} %add_convert_fusion.5), channel_id=1, source_target_pairs={{0,8},{4,12},{8,0},{12,4},{1,9},{5,13},{9,1},{13,5},{2,10},{6,14},... | collective-permute-start | bytes 2359304 | tf_op jit(solution)/shard_map/ppermute | solution.py:99
  101.1 19.3 %collective-permute-start.19 = (bf16[512,768]{1,0:T(8,128)(2,1)S(1)}, bf16[512,768]{1,0:T(8,128)(2,1)S(1)}, u32[]{:S(2)}, u32[]{:S(2)}) collective-permute-start(bf16[512,768]{1,0:T(8,128)(2,1)S(1)} %broadcast_select_fusion.12), channel_id=1, source_target_pairs={{0,4},{4,0},{8,12},{12,8},{1,5},{5,1},{9,13},{13,9},{2,6},{6,2},{1... | collective-permute-start | bytes 2359304 | tf_op jit(solution)/shard_map/ppermute | solution.py:98
  101.6 86.1 %collective-permute-start.26 = (bf16[512,768]{1,0:T(8,128)(2,1)S(1)}, bf16[512,768]{1,0:T(8,128)(2,1)S(1)}, u32[]{:S(2)}, u32[]{:S(2)}) collective-permute-start(bf16[512,768]{1,0:T(8,128)(2,1)S(1)} %add_convert_fusion.3), channel_id=1, source_target_pairs={{0,8},{4,12},{8,0},{12,4},{1,9},{5,13},{9,1},{13,5},{2,10},{6,14},... | collective-permute-start | bytes 2359304 | tf_op jit(solution)/shard_map/ppermute | solution.py:99
  120.7 28.2 %collective-permute-start.20 = (bf16[512,768]{1,0:T(8,128)(2,1)S(1)}, bf16[512,768]{1,0:T(8,128)(2,1)S(1)}, u32[]{:S(2)}, u32[]{:S(2)}) collective-permute-start(bf16[512,768]{1,0:T(8,128)(2,1)S(1)} %add_convert_fusion.4), channel_id=1, source_target_pairs={{0,8},{4,12},{8,0},{12,4},{1,9},{5,13},{9,1},{13,5},{2,10},{6,14},... | collective-permute-start | bytes 2359304 | tf_op jit(solution)/shard_map/ppermute | solution.py:99
  122.7 48.0 %collective-permute-start.18 = (bf16[512,768]{1,0:T(8,128)(2,1)S(1)}, bf16[512,768]{1,0:T(8,128)(2,1)S(1)}, u32[]{:S(2)}, u32[]{:S(2)}) collective-permute-start(bf16[512,768]{1,0:T(8,128)(2,1)S(1)} %fusion.93), channel_id=1, source_target_pairs={{0,4},{4,0},{8,12},{12,8},{1,5},{5,1},{9,13},{13,9},{2,6},{6,2},{1... | collective-permute-start | bytes 2359304 | tf_op jit(solution)/shard_map/ppermute | solution.py:106
  123.9 41.0 %collective-permute-start.29 = (bf16[512,768]{1,0:T(8,128)(2,1)S(1)}, bf16[512,768]{1,0:T(8,128)(2,1)S(1)}, u32[]{:S(2)}, u32[]{:S(2)}) collective-permute-start(bf16[512,768]{1,0:T(8,128)(2,1)S(1)} %add_convert_fusion.2), channel_id=1, source_target_pairs={{0,8},{4,12},{8,0},{12,4},{1,9},{5,13},{9,1},{13,5},{2,10},{6,14},... | collective-permute-start | bytes 2359304 | tf_op jit(solution)/shard_map/ppermute | solution.py:99
  154.0 14.5 %collective-permute-start.31 = (bf16[512,768]{1,0:T(8,128)(2,1)S(1)}, bf16[512,768]{1,0:T(8,128)(2,1)S(1)}, u32[]{:S(2)}, u32[]{:S(2)}) collective-permute-start(bf16[512,768]{1,0:T(8,128)(2,1)S(1)} %broadcast_select_fusion.5), channel_id=1, source_target_pairs={{0,4},{4,0},{8,12},{12,8},{1,5},{5,1},{9,13},{13,9},{2,6},{6,2},{1... | collective-permute-start | bytes 2359304 | tf_op jit(solution)/shard_map/ppermute | solution.py:98
  168.6 56.6 %collective-permute-start.30 = (bf16[512,768]{1,0:T(8,128)(2,1)S(1)}, bf16[512,768]{1,0:T(8,128)(2,1)S(1)}, u32[]{:S(2)}, u32[]{:S(2)}) collective-permute-start(bf16[512,768]{1,0:T(8,128)(2,1)S(1)} %get-tuple-element.68), channel_id=1, source_target_pairs={{0,4},{4,0},{8,12},{12,8},{1,5},{5,1},{9,13},{13,9},{2,6},{6,2},{1... | collective-permute-start | bytes 2359304 | tf_op jit(solution)/shard_map/ppermute | solution.py:106
  169.0 53.1 %collective-permute-start.32 = (bf16[512,768]{1,0:T(8,128)(2,1)S(1)}, bf16[512,768]{1,0:T(8,128)(2,1)}, u32[]{:S(2)}, u32[]{:S(2)}) collective-permute-start(bf16[512,768]{1,0:T(8,128)(2,1)S(1)} %add_convert_fusion.1), channel_id=1, source_target_pairs={{0,8},{4,12},{8,0},{12,4},{1,9},{5,13},{9,1},{13,5},{2,10},{6,14},... | collective-permute-start | bytes 2359304 | tf_op jit(solution)/shard_map/ppermute | solution.py:99
  187.7 12.3 %collective-permute-start.22 = (bf16[128,1536]{1,0:T(8,128)(2,1)S(1)}, bf16[128,1536]{1,0:T(8,128)(2,1)S(1)}, u32[]{:S(2)}, u32[]{:S(2)}) collective-permute-start(bf16[128,1536]{1,0:T(8,128)(2,1)S(1)} %slice.134), channel_id=1, source_target_pairs={{0,3},{1,0},{2,1},{3,2},{4,7},{5,4},{6,5},{7,6},{8,11},{9,8},{10,9... | collective-permute-start | bytes 1179656 | tf_op jit(solution)/shard_map/ppermute | solution.py:117
  196.4 8.0 %collective-permute-start.33 = (bf16[512,768]{1,0:T(8,128)(2,1)S(1)}, bf16[512,768]{1,0:T(8,128)(2,1)S(1)}, u32[]{:S(2)}, u32[]{:S(2)}) collective-permute-start(bf16[512,768]{1,0:T(8,128)(2,1)S(1)} %broadcast_select_fusion.4), channel_id=1, source_target_pairs={{0,4},{4,0},{8,12},{12,8},{1,5},{5,1},{9,13},{13,9},{2,6},{6,2},{1... | collective-permute-start | bytes 2359304 | tf_op jit(solution)/shard_map/ppermute | solution.py:98
  197.7 27.0 %collective-permute-start.27 = (bf16[512,768]{1,0:T(8,128)(2,1)S(1)}, bf16[512,768]{1,0:T(8,128)(2,1)S(1)}, u32[]{:S(2)}, u32[]{:S(2)}) collective-permute-start(bf16[512,768]{1,0:T(8,128)(2,1)S(1)} %fusion.108), channel_id=1, source_target_pairs={{0,4},{4,0},{8,12},{12,8},{1,5},{5,1},{9,13},{13,9},{2,6},{6,2},{1... | collective-permute-start | bytes 2359304 | tf_op jit(solution)/shard_map/ppermute | solution.py:106
  200.1 50.4 %collective-permute-start.23 = (bf16[128,1536]{1,0:T(8,128)(2,1)S(1)}, bf16[128,1536]{1,0:T(8,128)(2,1)}, u32[]{:S(2)}, u32[]{:S(2)}) collective-permute-start(bf16[128,1536]{1,0:T(8,128)(2,1)S(1)} %add_convert_fusion.11), channel_id=1, source_target_pairs={{0,3},{1,0},{2,1},{3,2},{4,7},{5,4},{6,5},{7,6},{8,11},{9,8},{10,9... | collective-permute-start | bytes 1179656 | tf_op jit(solution)/shard_map/ppermute | solution.py:117
  204.7 25.5 %collective-permute-start.35 = (bf16[512,768]{1,0:T(8,128)(2,1)S(1)}, bf16[512,768]{1,0:T(8,128)(2,1)}, u32[]{:S(2)}, u32[]{:S(2)}) collective-permute-start(bf16[512,768]{1,0:T(8,128)(2,1)S(1)} %add_convert_fusion), channel_id=1, source_target_pairs={{0,8},{4,12},{8,0},{12,4},{1,9},{5,13},{9,1},{13,5},{2,10},{6,14},... | collective-permute-start | bytes 2359304 | tf_op jit(solution)/shard_map/ppermute | solution.py:99
  224.6 8.6 %collective-permute-start.34 = (bf16[512,768]{1,0:T(8,128)(2,1)S(1)}, bf16[512,768]{1,0:T(8,128)(2,1)S(1)}, u32[]{:S(2)}, u32[]{:S(2)}) collective-permute-start(bf16[512,768]{1,0:T(8,128)(2,1)S(1)} %fusion.122), channel_id=1, source_target_pairs={{0,4},{4,0},{8,12},{12,8},{1,5},{5,1},{9,13},{13,9},{2,6},{6,2},{1... | collective-permute-start | bytes 2359304 | tf_op jit(solution)/shard_map/ppermute | solution.py:106
  250.5 12.0 %collective-permute-start.37 = (bf16[128,1536]{1,0:T(8,128)(2,1)S(1)}, bf16[128,1536]{1,0:T(8,128)(2,1)S(1)}, u32[]{:S(2)}, u32[]{:S(2)}) collective-permute-start(bf16[128,1536]{1,0:T(8,128)(2,1)S(1)} %get-tuple-element.66), channel_id=1, source_target_pairs={{0,3},{1,0},{2,1},{3,2},{4,7},{5,4},{6,5},{7,6},{8,11},{9,8},{10,9... | collective-permute-start | bytes 1179656 | tf_op jit(solution)/shard_map/ppermute | solution.py:117
  251.7 28.9 %collective-permute-start.24 = (bf16[128,1536]{1,0:T(8,128)(2,1)S(1)}, bf16[128,1536]{1,0:T(8,128)(2,1)S(1)}, u32[]{:S(2)}, u32[]{:S(2)}) collective-permute-start(bf16[128,1536]{1,0:T(8,128)(2,1)S(1)} %add_convert_fusion.10), channel_id=1, source_target_pairs={{0,3},{1,0},{2,1},{3,2},{4,7},{5,4},{6,5},{7,6},{8,11},{9,8},{10,9... | collective-permute-start | bytes 1179656 | tf_op jit(solution)/shard_map/ppermute | solution.py:117
  262.6 17.8 %collective-permute-start.38 = (bf16[128,1536]{1,0:T(8,128)(2,1)S(1)}, bf16[128,1536]{1,0:T(8,128)(2,1)S(1)}, u32[]{:S(2)}, u32[]{:S(2)}) collective-permute-start(bf16[128,1536]{1,0:T(8,128)(2,1)S(1)} %add_convert_fusion.8), channel_id=1, source_target_pairs={{0,3},{1,0},{2,1},{3,2},{4,7},{5,4},{6,5},{7,6},{8,11},{9,8},{10,9... | collective-permute-start | bytes 1179656 | tf_op jit(solution)/shard_map/ppermute | solution.py:117
  280.5 9.6 %collective-permute-start.39 = (bf16[128,1536]{1,0:T(8,128)(2,1)S(1)}, bf16[128,1536]{1,0:T(8,128)(2,1)S(1)}, u32[]{:S(2)}, u32[]{:S(2)}) collective-permute-start(bf16[128,1536]{1,0:T(8,128)(2,1)S(1)} %add_convert_fusion.7), channel_id=1, source_target_pairs={{0,3},{1,0},{2,1},{3,2},{4,7},{5,4},{6,5},{7,6},{8,11},{9,8},{10,9... | collective-permute-start | bytes 1179656 | tf_op jit(solution)/shard_map/ppermute | solution.py:117
  (15 other events, 263.4 us)
